TPU v7x, 32 devices: a whole 2x2x4 slice. The times are simulated.
32 devices in a mesh: groups: 2 (over y), node: 4 (over x, core), peer: 4 (over z).
Axes of the slice: x: 2, y: 2, z: 4, core: 2. Of those that a mesh axis runs over, the one named last changes fastest.
Arguments:
- moe_rows: bfloat16 [128, 7168], P(('groups', 'node', 'peer')), parts along dimension 0, may hold values from -6 to 6
- route_nodes: int32 [128, 2], P(('groups', 'node', 'peer')), parts along dimension 0, may hold values from 0 to 3, all different within a row; in each aligned block of 4 rows (0 to 3, 4 to 7, ...) at most 3 rows name the same one
- gates: bfloat16 [128, 2, 2], P(('groups', 'node', 'peer')), parts along dimension 0, may hold values from 0.049804688 to 0.5
- w_gate: bfloat16 [8, 7168, 2048], P('node', None, 'peer'), may hold values from -0.0625 to 0.0625
- w_up: bfloat16 [8, 7168, 2048], P('node', None, 'peer'), may hold values from -0.0625 to 0.0625
- w_down: bfloat16 [8, 2048, 7168], P('node', 'peer'), may hold values from -0.125 to 0.125
Outputs:
- moe_out: bfloat16 [128, 7168], P(('groups', 'node', 'peer')), parts along dimension 0
There are 2 independent parts, one for each index of `groups`. A program takes and returns all parts, laid end to end along the dimension named above; an argument that names none is the same for every part. Nothing has to cross between parts.
Inputs may be any that keep to these rules, and one draw needn't show every extreme that they name: `route_nodes`: each row names 2 different nodes; among the rows of one device no node is named by more than 3 rows, and in some devices' rows one node is named by exactly 3.
All inputs are finite; a program needn't handle non-finite values.
Results may differ from a plain program's by a relative error of at most 0.012.
Values may be sent and summed in bfloat16 or wider, within the bound.
A program may use at most 128 MiB of HBM per device.

v0:
```python
import jax
import jax.numpy as jnp
from jax import lax
from jax.sharding import PartitionSpec as P

EXP_NODE = 2
CAP = 3


def expert_work(slot_rows, slot_gates, w_gate, w_up, w_down):
    width = slot_rows.shape[-1]
    flat_rows = slot_rows.reshape(-1, width)
    flat_gates = slot_gates.reshape(-1, slot_gates.shape[-1]).astype(jnp.float32)
    accumulated = jnp.zeros(flat_rows.shape, jnp.float32)
    for expert_slot in range(EXP_NODE):
        gate_proj = jnp.dot(flat_rows, w_gate[expert_slot], preferred_element_type=jnp.float32)
        up_proj = jnp.dot(flat_rows, w_up[expert_slot], preferred_element_type=jnp.float32)
        hidden = (jax.nn.silu(gate_proj) * up_proj).astype(jnp.bfloat16)
        projected = jnp.dot(hidden, w_down[expert_slot], preferred_element_type=jnp.float32)
        accumulated = accumulated + flat_gates[:, expert_slot : expert_slot + 1] * projected
    return accumulated.astype(jnp.bfloat16).reshape(slot_rows.shape)


def on_device(moe_rows, route_nodes, gates, w_gate, w_up, w_down):
    node_count = lax.axis_size("node")
    peer_count = lax.axis_size("peer")
    width = moe_rows.shape[1]
    chosen = route_nodes[:, :, None] == jnp.arange(node_count, dtype=jnp.int32)[None, None, :]
    node_hits = jnp.sum(chosen.astype(jnp.int32), axis=1)
    before = jnp.cumsum(node_hits, axis=0) - node_hits
    placed = (node_hits[:, :, None] == 1) & (
        before[:, :, None] == jnp.arange(CAP, dtype=jnp.int32)[None, None, :]
    )
    placer = placed.astype(jnp.bfloat16)
    sent_rows = jnp.einsum(
        "rkc,rd->kcd", placer, moe_rows, preferred_element_type=jnp.float32
    ).astype(jnp.bfloat16)
    node_gates = jnp.einsum("rjk,rje->rke", chosen.astype(jnp.float32), gates.astype(jnp.float32))
    sent_gates = jnp.einsum("rkc,rke->kce", placed.astype(jnp.float32), node_gates).astype(
        jnp.bfloat16
    )
    wide_rows = jnp.broadcast_to(sent_rows[:, None], (node_count, peer_count, CAP, width))
    wide_gates = jnp.broadcast_to(sent_gates[:, None], (node_count, peer_count, CAP, EXP_NODE))
    wide_rows = wide_rows.reshape(node_count * peer_count, CAP, width)
    wide_gates = wide_gates.reshape(node_count * peer_count, CAP, EXP_NODE)
    got_rows, got_gates = (
        lax.all_to_all(wide_rows, ("node", "peer"), split_axis=0, concat_axis=0, tiled=True),
        lax.all_to_all(wide_gates, ("node", "peer"), split_axis=0, concat_axis=0, tiled=True),
    )
    slot_rows = got_rows.reshape(node_count, peer_count, CAP, width)
    slot_gates = got_gates.reshape(node_count, peer_count, CAP, EXP_NODE)
    partial_value = expert_work(slot_rows, slot_gates, w_gate, w_up, w_down)
    summed = lax.psum_scatter(partial_value, "peer", scatter_dimension=1, tiled=True).astype(
        jnp.float32
    )
    node_out = summed.astype(jnp.bfloat16)[:, 0]
    returned = lax.all_to_all(node_out, "node", split_axis=0, concat_axis=0, tiled=True)
    moe_out = jnp.einsum(
        "rkc,kcd->rd", placer, returned, preferred_element_type=jnp.float32
    ).astype(jnp.bfloat16)
    return moe_out


def solution(mesh):
    in_specs = (
        P(("groups", "node", "peer"), None),
        P(("groups", "node", "peer"), None),
        P(("groups", "node", "peer"), None, None),
        P("node", None, "peer"),
        P("node", None, "peer"),
        P("node", "peer", None),
    )
    out_specs = P(("groups", "node", "peer"), None)
    return jax.shard_map(
        on_device, mesh=mesh, in_specs=in_specs, out_specs=out_specs, check_vma=False
    )
```

profile of v0, /device:TPU:0, one launch (start us, length us, event | category | flops | bytes accessed | tf_op | source)
XLA Modules:
  0.0 139.1 jit_solution(17588486469696676940)
XLA Ops:
  6.5 0.8 copy.45
  7.5 0.1 copy.47
  7.6 0.8 copy.46
  8.4 0.2 fusion.50
  8.7 0.1 fusion.54
  8.8 0.6 broadcast_in_dim.4.clone
  9.4 7.4 %all-to-all-start = ((bf16[16,3,2]{1,2,0:T(2,128)(2,1)}), bf16[16,3,2]{1,2,0:T(2,128)(2,1)S(1)}, u32[]{:S(2)}, u32[]{:S(2)}) async-start(bf16[16,3,2]{1,2,0:T(2,128)(2,1)} %bitcast), calls=%async_computation | async-start | bytes 16384 | tf_op jit(solution)/shard_map/all_to_all | solution.py:48
  16.8 0.3 convolution_convert_fusion
  17.2 5.8 %all-to-all-done = bf16[16,3,2]{1,2,0:T(2,128)(2,1)S(1)} async-done(((bf16[16,3,2]{1,2,0:T(2,128)(2,1)}), bf16[16,3,2]{1,2,0:T(2,128)(2,1)S(1)}, u32[]{:S(2)}, u32[]{:S(2)}) %all-to-all-start) | async-done | bytes 224 | tf_op jit(solution)/shard_map/all_to_all | solution.py:48
  23.1 1.2 broadcast_in_dim.5
  24.3 3.6 %all-to-all-start.1 = ((bf16[16,3,7168]{2,1,0:T(4,128)(2,1)}), bf16[16,3,7168]{2,1,0:T(4,128)(2,1)S(1)}, u32[]{:S(2)}, u32[]{:S(2)}) async-start(bf16[16,3,7168]{2,1,0:T(4,128)(2,1)} %bitcast.3), calls=%async_computation.1 | async-start | bytes 1835008 | tf_op jit(solution)/shard_map/all_to_all | solution.py:47
  28.3 23.8 %all-to-all-done.1 = bf16[16,3,7168]{2,1,0:T(4,128)(2,1)S(1)} async-done(((bf16[16,3,7168]{2,1,0:T(4,128)(2,1)}), bf16[16,3,7168]{2,1,0:T(4,128)(2,1)S(1)}, u32[]{:S(2)}, u32[]{:S(2)}) %all-to-all-start.1) | async-done | bytes 688160 | tf_op jit(solution)/shard_map/all_to_all | solution.py:47
  52.0 0.6 reshape_reshape.4
  52.6 4.4 %fusion.11 = f32[48,512]{1,0:T(8,128)S(1)} fusion(bf16[48,7168]{1,0:T(8,128)(2,1)S(1)} %reshape_reshape.4, bf16[2,7168,512]{2,1,0:T(8,128)(2,1)} %param.9), kind=kOutput, calls=%fused_computation.15 | convolution fusion | flops 352321536 | bytes 8126464 | tf_op jit(solution)/shard_map/dot_general | solution.py:16
  57.0 4.4 %fusion.6 = f32[48,512]{1,0:T(8,128)S(1)} fusion(bf16[48,7168]{1,0:T(8,128)(2,1)S(1)} %reshape_reshape.4, bf16[2,7168,512]{2,1,0:T(8,128)(2,1)} %param.9), kind=kOutput, calls=%fused_computation.10 | convolution fusion | flops 352321536 | bytes 8126464 | tf_op jit(solution)/shard_map/dot_general | solution.py:16
  61.5 9.2 %convolution_multiply_fusion.1 = f32[48,7168]{1,0:T(8,128)} fusion(bf16[2,512,7168]{2,1,0:T(8,128)(2,1)} %param.11, f32[48]{0:T(128)S(1)} %get-tuple-element.6, bf16[48,7168]{1,0:T(8,128)(2,1)S(1)} %reshape_reshape.4, bf16[2,7168,512]{2,1,0:T(8,128)(2,1)} %param.10, f32[48,512]{1,0:T(8,128)S(1)} %fusion.11), kind=kOutput, calls=%fused_computation.2 | convolution fusion | flops 705134592 | bytes 16842944 | tf_op jit(solution)/shard_map/dot_general | solution.py:19
  70.7 8.4 %fusion.1 = bf16[48,7168]{1,0:T(8,128)(2,1)S(1)} fusion(f32[48,7168]{1,0:T(8,128)} %convolution_multiply_fusion.1, bf16[2,512,7168]{2,1,0:T(8,128)(2,1)} %param.11, f32[48]{0:T(128)S(1)} %get-tuple-element.5, bf16[48,7168]{1,0:T(8,128)(2,1)S(1)} %reshape_reshape.4, bf16[2,7168,512]{2,1,0:T(8,128)(2,1)} %param.10, f32[48,512]{1,0:T(8,128)S(1)} %fusion.6), kind=kOutput, calls=%fused_computation.3 | convolution fusion | flops 705822720 | bytes 17531072 | tf_op jit(solution)/shard_map/dot_general | solution.py:19
  79.2 0.4 reshape.29
  79.6 1.5 %copy.55 = bf16[4,4,3,7168]{3,0,2,1:T(4,128)(2,1)} copy(bf16[4,4,3,7168]{3,2,1,0:T(4,128)(2,1)S(1)} %reshape.29) | data formatting | bytes 1376256 | tf_op jit(solution)/shard_map/reshape | solution.py:21
  81.2 0.6 dynamic-slice
  81.7 39.6 %all-reduce.3.cloned.1.call-done = bf16[4,4,3,7168]{3,0,2,1:T(4,128)(2,1)} async-done(((bf16[4,4,3,7168]{3,0,2,1:T(4,128)(2,1)}), bf16[4,4,3,7168]{3,0,2,1:T(4,128)(2,1)}) %all-reduce.3.cloned.1.call-update) | async-done | bytes 688144
  121.3 1.6 %dynamic-slice_bitcast_fusion = bf16[4,3,7168]{2,0,1:T(4,128)(2,1)S(1)} fusion(bf16[4,4,3,7168]{3,0,2,1:T(4,128)(2,1)} %all-reduce.3.cloned.1.call-done, u32[]{:T(128)} %bitcast.13), kind=kLoop, calls=%fused_computation.28 | loop fusion | bytes 344068 | tf_op jit(solution)/shard_map/squeeze | solution.py:56
  123.1 8.2 %all_to_all.15 = bf16[4,3,7168]{2,1,0:T(4,128)(2,1)S(1)} all-to-all(bf16[4,3,7168]{2,1,0:T(4,128)(2,1)S(1)} %copy.56), channel_id=1, replica_groups=mesh['groups'=2,'node'=4,'peer'=4] {'node'}, dimensions={0} | all-to-all | bytes 344064 | tf_op jit(solution)/shard_map/all_to_all | solution.py:57
  131.3 0.9 fusion.2
  (18 shorter events, 0.9 us)
Async XLA Ops:
  6.5 10.2 %copy-start = (bf16[4,7168]{1,0:T(4,128)(2,1)S(1)}, bf16[4,7168]{1,0:T(4,128)(2,1)}, u32[]{:S(2)}) copy-start(bf16[4,7168]{1,0:T(4,128)(2,1)} %param.6) | copy-start | bytes 172036
  9.4 13.7 %all-to-all-start = ((bf16[16,3,2]{1,2,0:T(2,128)(2,1)}), bf16[16,3,2]{1,2,0:T(2,128)(2,1)S(1)}, u32[]{:S(2)}, u32[]{:S(2)}) async-start(bf16[16,3,2]{1,2,0:T(2,128)(2,1)} %bitcast), calls=%async_computation | async-start | bytes 16384 | tf_op jit(solution)/shard_map/all_to_all | solution.py:48
  24.3 27.8 %all-to-all-start.1 = ((bf16[16,3,7168]{2,1,0:T(4,128)(2,1)}), bf16[16,3,7168]{2,1,0:T(4,128)(2,1)S(1)}, u32[]{:S(2)}, u32[]{:S(2)}) async-start(bf16[16,3,7168]{2,1,0:T(4,128)(2,1)} %bitcast.3), calls=%async_computation.1 | async-start | bytes 1835008 | tf_op jit(solution)/shard_map/all_to_all | solution.py:47
  27.9 93.4 %all-reduce.3.cloned.1.call-start = ((), (), s32[]{:S(2)}) async-start(), calls=%async_computation.3 | async-start | bytes 1376256
  70.7 10.4 %copy-start.1 = (u32[32]{0:T(128)S(1)}, u32[32]{0:T(128)}, u32[]{:S(2)}) copy-start(u32[32]{0:T(128)} %constant.19) | copy-start | bytes 388
Sparse Core Ops, SparseCore 0:
  81.3 40.0 all-reduce.2
where the time goes:
time: 140 us; the launch traced here: 139 us
  waiting for transfers between devices  69.2 us (49%)
  matrix products  28.1 us (20%)
  between operations  13.5 us (10%)
  starting transfers between devices  11 us (8%)
  local copies, waits for them, and re-layouts  8.88 us (6%)
  blocking collectives  8.23 us (6%)
    unnamed x2, waiting for transfers between devices  39.6 us
    all_to_all x1, waiting for transfers between devices, on_device(): lax.all_to_all(wide_rows, ('node', 'peer'), split_axis=0, concat_axis=0,...  23.8 us
    dot_general x2, matrix products, expert_work(): jnp.dot(hidden, w_down[expert_slot], preferred_element_type=jnp.float32)  17.7 us
    dot_general x2, matrix products, expert_work(): jnp.dot(flat_rows, w_gate[expert_slot], preferred_element_type=jnp.float32)  8.87 us
    all_to_all x1, blocking collectives, on_device(): lax.all_to_all(node_out, 'node', split_axis=0, concat_axis=0, tiled=True)  8.23 us
    all_to_all x1, starting transfers between devices, on_device(): lax.all_to_all(wide_gates, ('node', 'peer'), split_axis=0, concat_axis=0,...  7.36 us
    all_to_all x1, waiting for transfers between devices, on_device(): lax.all_to_all(wide_gates, ('node', 'peer'), split_axis=0, concat_axis=0,...  5.85 us
    all_to_all x1, starting transfers between devices, on_device(): lax.all_to_all(wide_rows, ('node', 'peer'), split_axis=0, concat_axis=0,...  3.63 us
  transfers between devices with their start and end apart: 3, of which 3 were waited for; matrix products, arithmetic and copies ran while one was open for 1% of the time, Pallas kernels for 0%

commit v1 on v0

v1 whole, which is shorter than its diff:
```python
import functools

import jax
import jax.numpy as jnp
from jax import lax
from jax.experimental import pallas as pl
from jax.experimental.pallas import tpu as pltpu
from jax.sharding import PartitionSpec as P

MESH = pl.DeviceIdType.MESH
EXP_NODE = 2
CORES = 2
SLOT = 16
GATE_COLS = 128
CHUNKS_IN = 2
CHUNKS_OUT = 2
F32 = jnp.float32
BF16 = jnp.bfloat16


def kernel(
    peers, xs, rows, chunks_in, chunks_out,
    x_ref, g_ref, wg_hbm, wu_hbm, wd_hbm, out_ref,
    wg, wu, wd, zin, gin, zgate, ggate, acc, hid,
    part, cbuf, xsum, xbuf, zout, zbuf,
    w_sem, d_sem,
    zs, zr, xs_s, xs_r, cs, cr,
    gzs, gzr, gxs, gxr, gcs, gcr,
    ocs, ocr, oxs, oxr, ozs, ozr,
):
    width = x_ref.shape[1]
    pieces = SLOT // rows
    node_rows = peers * rows
    node = lax.axis_index("node")
    p = lax.axis_index("peer")
    c = lax.rem(node, CORES)
    xi = lax.div(node, CORES)

    w_in = width // chunks_in
    v_in = w_in // pieces
    w_out = width // chunks_out
    v_out = w_out // pieces

    weight_copies = []
    for t in range(chunks_in):
        both = []
        for i, (src, dst) in enumerate(((wg_hbm, wg), (wu_hbm, wu))):
            span = pl.ds(t * w_in, w_in)
            copy = pltpu.make_async_copy(src.at[:, span, :], dst.at[:, span, :], w_sem.at[t, i])
            copy.start()
            both.append(copy)
        weight_copies.append(both)
    down_copies = []
    for t in range(chunks_out):
        span = pl.ds(t * w_out, w_out)
        copy = pltpu.make_async_copy(wd_hbm.at[:, :, span], wd.at[:, :, span], d_sem.at[t])
        copy.start()
        down_copies.append(copy)

    def peer_of(d):
        return lax.rem(p + d, peers)

    def x_of(d):
        return lax.rem(xi + d, xs)

    barrier = pltpu.get_barrier_semaphore()
    for d in range(1, peers):
        pl.semaphore_signal(barrier, inc=1, device_id={"peer": peer_of(d)}, device_id_type=MESH)
    for d in range(1, xs):
        pl.semaphore_signal(
            barrier, inc=1, device_id={"node": x_of(d) * CORES + c}, device_id_type=MESH
        )
    pl.semaphore_signal(
        barrier, inc=1, device_id={"node": xi * CORES + 1 - c}, device_id_type=MESH
    )

    for t in range(chunks_in):
        own = [
            x_ref[:, t * w_in + j * v_in : t * w_in + (j + 1) * v_in].astype(F32)
            for j in range(pieces)
        ]
        zin[t, p] = jnp.concatenate(own, axis=0).astype(BF16)
    zgate[p] = jnp.concatenate([g_ref[...]] * pieces, axis=0).astype(BF16)

    pl.semaphore_wait(barrier, peers - 1 + xs - 1 + 1)

    sends = []

    def send(src, dst, ssem, rsem, where):
        copy = pltpu.make_async_remote_copy(
            src_ref=src, dst_ref=dst, send_sem=ssem, recv_sem=rsem,
            device_id=where, device_id_type=MESH,
        )
        copy.start()
        sends.append(copy)

    def arrived(dst, ssem, rsem, where):
        pltpu.make_async_remote_copy(
            src_ref=dst, dst_ref=dst, send_sem=ssem, recv_sem=rsem,
            device_id=where, device_id_type=MESH,
        ).wait_recv()

    def to_peer(d):
        return {"peer": peer_of(d)}

    def to_x(d):
        return {"node": x_of(d) * CORES + c}

    to_core = {"node": xi * CORES + 1 - c}

    for t in range(chunks_in):
        for d in range(1, peers):
            send(zin.at[t, p], zin.at[t, p], zs.at[t, d - 1], zr.at[t, d - 1], to_peer(d))
    for d in range(1, peers):
        send(zgate.at[p], zgate.at[p], gzs.at[d - 1], gzr.at[d - 1], to_peer(d))

    row_at = lax.broadcasted_iota(jnp.int32, (node_rows, peers * SLOT), 0)
    col_at = lax.broadcasted_iota(jnp.int32, (node_rows, peers * SLOT), 1)
    row_base = (row_at // rows) * SLOT + row_at % rows

    def spread(j):
        return jnp.where(col_at == row_base + j * rows, 1.0, 0.0).astype(BF16)

    def place(t):
        for d in range(1, peers):
            arrived(zin.at[t, peer_of(peers - d)], zs.at[t, d - 1], zr.at[t, d - 1], to_peer(d))
        stacked = zin[t].reshape(peers * SLOT, v_in)
        for j in range(pieces):
            gin[t, c, xi, :, j * v_in : (j + 1) * v_in] = jnp.dot(
                spread(j), stacked, preferred_element_type=F32
            ).astype(BF16)
        for d in range(1, xs):
            send(gin.at[t, c, xi], gin.at[t, c, xi], xs_s.at[t, d - 1], xs_r.at[t, d - 1], to_x(d))
        send(gin.at[t, c, xi], gin.at[t, c, xi], cs.at[t, 0], cr.at[t, 0], to_core)

    def forward(t):
        for d in range(1, xs):
            other = x_of(xs - d)
            block = gin.at[t, c, other]
            arrived(block, xs_s.at[t, d - 1], xs_r.at[t, d - 1], to_x(d))
            send(block, block, cs.at[t, d], cr.at[t, d], to_core)

    def gathered(t):
        for d in range(xs):
            block = gin.at[t, 1 - c, x_of(xs - d)]
            arrived(block, cs.at[t, d], cr.at[t, d], to_core)

    all_rows = CORES * xs * node_rows

    def first_half(t):
        gathered(t)
        for copy in weight_copies[t]:
            copy.wait()
        lhs = gin[t].reshape(all_rows, w_in)
        for e in range(EXP_NODE):
            for i, w in enumerate((wg, wu)):
                value = jnp.dot(
                    lhs, w[e, t * w_in : (t + 1) * w_in, :], preferred_element_type=F32
                )
                if t == 0:
                    acc[e, i] = value
                else:
                    acc[e, i] += value

    for t in range(chunks_in):
        place(t)

    for d in range(1, peers):
        arrived(zgate.at[peer_of(peers - d)], gzs.at[d - 1], gzr.at[d - 1], to_peer(d))
    ggate[c, xi] = jnp.dot(
        spread(0), zgate[...].reshape(peers * SLOT, GATE_COLS), preferred_element_type=F32
    ).astype(BF16)
    own_gates = ggate.at[c, xi]
    for d in range(1, xs):
        send(own_gates, own_gates, gxs.at[d - 1], gxr.at[d - 1], to_x(d))
    send(own_gates, own_gates, gcs.at[0], gcr.at[0], to_core)

    forward(0)
    for t in range(chunks_in):
        if t + 1 < chunks_in:
            forward(t + 1)
        else:
            for d in range(1, xs):
                block = ggate.at[c, x_of(xs - d)]
                arrived(block, gxs.at[d - 1], gxr.at[d - 1], to_x(d))
                send(block, block, gcs.at[d], gcr.at[d], to_core)
        first_half(t)

    for d in range(xs):
        arrived(ggate.at[1 - c, x_of(xs - d)], gcs.at[d], gcr.at[d], to_core)
    every_gate = ggate[...].reshape(all_rows, GATE_COLS).astype(F32)
    gate_col = lax.broadcasted_iota(jnp.int32, (all_rows, GATE_COLS), 1)
    row_gates = []
    for e in range(EXP_NODE):
        picked = jnp.where(gate_col == node * EXP_NODE + e, every_gate, 0.0)
        row_gates.append(jnp.sum(picked, axis=1, keepdims=True))
        gate_proj = acc[e, 0]
        hid[e] = (gate_proj / (1.0 + jnp.exp(-gate_proj)) * acc[e, 1]).astype(BF16)

    def second_half(t):
        down_copies[t].wait()
        total = None
        for e in range(EXP_NODE):
            value = row_gates[e] * jnp.dot(
                hid[e], wd[e, :, t * w_out : (t + 1) * w_out], preferred_element_type=F32
            )
            total = value if total is None else total + value
        part[t] = total.astype(BF16).reshape(CORES, xs, node_rows, w_out)
        send(part.at[t, 1 - c], cbuf.at[t], ocs.at[t], ocr.at[t], to_core)

    def core_sum(t):
        arrived(cbuf.at[t], ocs.at[t], ocr.at[t], to_core)
        xsum[t] = (part[t, c].astype(F32) + cbuf[t].astype(F32)).astype(BF16)
        for d in range(1, xs):
            send(
                xsum.at[t, x_of(d)], xbuf.at[t, d - 1],
                oxs.at[t, d - 1], oxr.at[t, d - 1], to_x(d),
            )

    row_of = lax.broadcasted_iota(jnp.int32, (peers * SLOT, node_rows), 1)
    slot_of = lax.broadcasted_iota(jnp.int32, (peers * SLOT, node_rows), 0)
    slot_base = (row_of // rows) * SLOT + row_of % rows

    def node_sum(t):
        value = xsum[t, xi].astype(F32)
        for d in range(1, xs):
            arrived(xbuf.at[t, d - 1], oxs.at[t, d - 1], oxr.at[t, d - 1], to_x(d))
            value = value + xbuf[t, d - 1].astype(F32)
        value = value.astype(BF16)
        slots = None
        for j in range(pieces):
            gather = jnp.where(slot_of == slot_base + j * rows, 1.0, 0.0).astype(BF16)
            piece = jnp.dot(
                gather, value[:, j * v_out : (j + 1) * v_out], preferred_element_type=F32
            )
            slots = piece if slots is None else slots + piece
        zout[t] = slots.astype(BF16).reshape(peers, SLOT, v_out)
        for d in range(1, peers):
            send(
                zout.at[t, peer_of(d)], zbuf.at[t, d - 1],
                ozs.at[t, d - 1], ozr.at[t, d - 1], to_peer(d),
            )

    def finish(t):
        value = zout[t, p].astype(F32)
        for d in range(1, peers):
            arrived(zbuf.at[t, d - 1], ozs.at[t, d - 1], ozr.at[t, d - 1], to_peer(d))
            value = value + zbuf[t, d - 1].astype(F32)
        for j in range(pieces):
            out_ref[:, t * w_out + j * v_out : t * w_out + (j + 1) * v_out] = value[
                j * rows : (j + 1) * rows
            ].astype(BF16)

    steps = (second_half, core_sum, node_sum, finish)
    for t in range(chunks_out + len(steps) - 1):
        for lag, step in enumerate(steps):
            if 0 <= t - lag < chunks_out:
                step(t - lag)

    for copy in sends:
        copy.wait_send()


def on_device(moe_rows, route_nodes, gates, w_gate, w_up, w_down):
    node_count = lax.axis_size("node")
    peers = lax.axis_size("peer")
    xs = node_count // CORES
    rows, width = moe_rows.shape
    hidden = w_gate.shape[2]
    pieces = SLOT // rows
    node_rows = peers * rows
    all_rows = node_count * node_rows
    ti, to = CHUNKS_IN, CHUNKS_OUT
    wi, wo = width // ti, width // to
    vi, vo = wi // pieces, wo // pieces

    column = jnp.arange(GATE_COLS, dtype=jnp.int32)[None, :]
    gate_matrix = jnp.zeros((rows, GATE_COLS), F32)
    for j in range(route_nodes.shape[1]):
        for e in range(EXP_NODE):
            hit = column == route_nodes[:, j : j + 1] * EXP_NODE + e
            gate_matrix = jnp.where(hit, gates[:, j, e : e + 1].astype(F32), gate_matrix)

    vmem = pl.BlockSpec(memory_space=pltpu.VMEM)
    hbm = pl.BlockSpec(memory_space=pl.ANY)
    dma = pltpu.SemaphoreType.DMA
    far = max(peers - 1, 1)
    xfar = max(xs - 1, 1)
    scratch = [
        pltpu.VMEM(w_gate.shape, BF16),
        pltpu.VMEM(w_up.shape, BF16),
        pltpu.VMEM(w_down.shape, BF16),
        pltpu.VMEM((ti, peers, SLOT, vi), BF16),
        pltpu.VMEM((ti, CORES, xs, node_rows, wi), BF16),
        pltpu.VMEM((peers, SLOT, GATE_COLS), BF16),
        pltpu.VMEM((CORES, xs, node_rows, GATE_COLS), BF16),
        pltpu.VMEM((EXP_NODE, 2, all_rows, hidden), F32),
        pltpu.VMEM((EXP_NODE, all_rows, hidden), BF16),
        pltpu.VMEM((to, CORES, xs, node_rows, wo), BF16),
        pltpu.VMEM((to, xs, node_rows, wo), BF16),
        pltpu.VMEM((to, xs, node_rows, wo), BF16),
        pltpu.VMEM((to, xfar, node_rows, wo), BF16),
        pltpu.VMEM((to, peers, SLOT, vo), BF16),
        pltpu.VMEM((to, far, SLOT, vo), BF16),
        dma((ti, 2)), dma((to,)),
        dma((ti, far)), dma((ti, far)), dma((ti, xfar)), dma((ti, xfar)),
        dma((ti, xs)), dma((ti, xs)),
        dma((far,)), dma((far,)), dma((xfar,)), dma((xfar,)), dma((xs,)), dma((xs,)),
        dma((to,)), dma((to,)), dma((to, xfar)), dma((to, xfar)), dma((to, far)), dma((to, far)),
    ]
    weight_count = w_gate.size + w_up.size + w_down.size
    return pl.pallas_call(
        functools.partial(kernel, peers, xs, rows, ti, to),
        out_shape=jax.ShapeDtypeStruct((rows, width), BF16),
        in_specs=[vmem, vmem, hbm, hbm, hbm],
        out_specs=vmem,
        scratch_shapes=scratch,
        compiler_params=pltpu.CompilerParams(
            collective_id=0, has_side_effects=True, vmem_limit_bytes=60 * 1024 * 1024
        ),
        cost_estimate=pl.CostEstimate(
            flops=2 * all_rows * weight_count,
            bytes_accessed=2 * weight_count,
            transcendentals=EXP_NODE * all_rows * hidden,
        ),
    )(moe_rows, gate_matrix, w_gate, w_up, w_down)


def solution(mesh):
    in_specs = (
        P(("groups", "node", "peer"), None),
        P(("groups", "node", "peer"), None),
        P(("groups", "node", "peer"), None, None),
        P("node", None, "peer"),
        P("node", None, "peer"),
        P("node", "peer", None),
    )
    out_specs = P(("groups", "node", "peer"), None)
    return jax.shard_map(
        on_device, mesh=mesh, in_specs=in_specs, out_specs=out_specs, check_vma=False
    )
```

time: 140 us -> 40.4 us (0.29)
  waiting for transfers between devices: 69.2 us -> 0 us
  Pallas kernels: 0 us -> 36.6 us
  matrix products: 28.1 us -> 0 us
  between operations: 13.5 us -> 0.01 us
  starting transfers between devices: 11 us -> 0 us
  blocking collectives: 8.23 us -> 0 us
  local copies, waits for them, and re-layouts: 8.88 us -> 1.46 us
  other arithmetic: 0.15 us -> 2.15 us
    unnamed x2 -> x0, waiting for transfers between devices: 39.6 us -> none
    pallas_call x0 -> x1, Pallas kernels: none -> 36.6 us  [on_device(): pl.pallas_call(functools.partial(kernel, peers, xs, rows, ti, to), out_sh...]
    all_to_all x2 -> x0, waiting for transfers between devices: 29.6 us -> none  [the longest x1 23.8 us: on_device(): lax.all_to_all(wide_rows, ('node', 'peer'), split_axis=0, concat_axis=0,...]
    dot_general x8 -> x0, matrix products: 28.1 us -> none  [the longest x2 17.7 us: expert_work(): jnp.dot(hidden, w_down[expert_slot], preferred_element_type=jnp.float32)]
    all_to_all x2 -> x0, starting transfers between devices: 11 us -> none  [the longest x1 7.36 us: on_device(): lax.all_to_all(wide_gates, ('node', 'peer'), split_axis=0, concat_axis=0,...]
    all_to_all x1 -> x0, blocking collectives: 8.23 us -> none  [on_device(): lax.all_to_all(node_out, 'node', split_axis=0, concat_axis=0, tiled=True)]
    reshape x2 -> x0, local copies, waits for them, and re-layouts: 1.94 us -> none  [expert_work(): return accumulated.astype(jnp.bfloat16).reshape(slot_rows.shape)]
    broadcast_in_dim x2 -> x0, local copies, waits for them, and re-layouts: 1.78 us -> none  [the longest x1 1.18 us: on_device(): jnp.broadcast_to(sent_rows[:, None], (node_count, peer_count, CAP, width))]
  transfers between devices with their start and end apart: 3 -> 0, of which waited for: 3 -> 0; matrix products, arithmetic and copies ran while one was open for 1% -> 0% of each run, Pallas kernels for 0% -> 0%
where the time goes in v1:
time: 40.4 us; the launch traced here: 40.2 us
  Pallas kernels  36.6 us (91%)
  other arithmetic  2.15 us (5%)
  local copies, waits for them, and re-layouts  1.46 us (4%)
    pallas_call x1, Pallas kernels, on_device(): pl.pallas_call(functools.partial(kernel, peers, xs, rows, ti, to), out_sh...  36.6 us
    unnamed x1, local copies, waits for them, and re-layouts  1.46 us

profile of v1, /device:TPU:0, one launch (start us, length us, event | category | flops | bytes accessed | tf_op | source)
XLA Modules:
  0.0 40.2 jit_solution(14524939116712674292)
XLA Ops:
  0.0 0.8 %add_bitcast_fusion.1 = (s32[4]{0:T(128)S(1)}, s32[4]{0:T(128)S(1)}, s32[4]{0:T(128)S(1)}, s32[4]{0:T(128)S(1)}) fusion(s32[4,2]{0,1:T(2,128)} %param.7), kind=kLoop, calls=%fused_computation.11 | loop fusion | flops 16 | bytes 96 | tf_op jit(solution)/shard_map/eq | solution.py:281
  0.8 0.7 %bitcast_convert_fusion.3 = (f32[4]{0:T(128)S(1)}, f32[4]{0:T(128)S(1)}, f32[4]{0:T(128)S(1)}, f32[4]{0:T(128)S(1)}) fusion(bf16[4,2,2]{0,2,1:T(2,128)(2,1)} %param.8), kind=kLoop, calls=%fused_computation.8 | loop fusion | flops 16 | bytes 96 | tf_op jit(solution)/shard_map/convert_element_type | solution.py:282
  1.5 0.7 %select_select_fusion.g_ref = f32[4,128]{1,0:T(4,128)} fusion(f32[4]{0:T(128)S(1)} %get-tuple-element.11, s32[4]{0:T(128)S(1)} %get-tuple-element.6, f32[4]{0:T(128)S(1)} %get-tuple-element.12, s32[4]{0:T(128)S(1)} %get-tuple-element.8, f32[4]{0:T(128)S(1)} %get-tuple-element.10, s32[4]{0:T(128)S(1)} %get-tuple-element.7, f32[4]{0:T(128)S(1)} %get-tuple-element.9, ...), kind=kLoop, calls=%fused_computation | loop fusion | flops 4096 | bytes 2176 | tf_op jit(solution)/shard_map/jit(_where)/select_n | solution.py:282
  2.2 36.6 %shard_map.64 = bf16[4,7168]{1,0:T(4,128)(2,1)} custom-call(bf16[4,7168]{1,0:T(4,128)(2,1)} %x_ref.1, f32[4,128]{1,0:T(4,128)} %select_select_fusion.g_ref, bf16[2,7168,512]{2,1,0:T(8,128)(2,1)} %wg_hbm.1, bf16[2,7168,512]{2,1,0:T(8,128)(2,1)} %wu_hbm.1, bf16[2,512,7168]{2,1,0:T(8,128)(2,1)} %wd_hbm.1), custom_call_target="tpu_custom_call" | custom-call | flops 2818572288 | bytes 44040192 | tf_op jit(solution)/shard_map/pallas_call | solution.py:312
  38.7 1.5 %copy.8 = bf16[4,7168]{1,0:T(4,128)(2,1)} copy(bf16[4,7168]{1,0:T(4,128)(2,1)} %shard_map.64) | data formatting | bytes 114688

commit v2 on v1

--- a/solution.py
+++ b/solution.py
@@ -12,23 +12,32 @@
 CORES = 2
 SLOT = 16
 GATE_COLS = 128
-CHUNKS_IN = 2
-CHUNKS_OUT = 2
+UNIT = 512
+PARTS_IN = 4
+PARTS_OUT = 4
+LAGS = (0, 1, 3, 5)
 F32 = jnp.float32
 BF16 = jnp.bfloat16
 
 
+def chunks_of(width, parts):
+    units = width // UNIT
+    parts = min(parts, units)
+    edges = [UNIT * (units * k // parts) for k in range(parts + 1)]
+    return [(a, b - a) for a, b in zip(edges[:-1], edges[1:])]
+
+
 def kernel(
-    peers, xs, rows, chunks_in, chunks_out,
-    x_ref, g_ref, wg_hbm, wu_hbm, wd_hbm, out_ref,
-    wg, wu, wd, zin, gin, zgate, ggate, acc, hid,
-    part, cbuf, xsum, xbuf, zout, zbuf,
+    peers, xs, rows, spans_in, spans_out,
+    x_ref, r_ref, g_ref, wg_hbm, wu_hbm, wd_hbm, out_ref,
+    wg, wu, wd, zins, gins, zgate, ggate, acc, hid,
+    parts, cbufs, xsums, xbufs, zouts, zbufs,
     w_sem, d_sem,
     zs, zr, xs_s, xs_r, cs, cr,
     gzs, gzr, gxs, gxr, gcs, gcr,
     ocs, ocr, oxs, oxr, ozs, ozr,
 ):
-    width = x_ref.shape[1]
+    chunks_in, chunks_out = len(spans_in), len(spans_out)
     pieces = SLOT // rows
     node_rows = peers * rows
     node = lax.axis_index("node")
@@ -36,23 +45,18 @@
     c = lax.rem(node, CORES)
     xi = lax.div(node, CORES)
 
-    w_in = width // chunks_in
-    v_in = w_in // pieces
-    w_out = width // chunks_out
-    v_out = w_out // pieces
-
     weight_copies = []
     for t in range(chunks_in):
         both = []
         for i, (src, dst) in enumerate(((wg_hbm, wg), (wu_hbm, wu))):
-            span = pl.ds(t * w_in, w_in)
+            span = pl.ds(*spans_in[t])
             copy = pltpu.make_async_copy(src.at[:, span, :], dst.at[:, span, :], w_sem.at[t, i])
             copy.start()
             both.append(copy)
         weight_copies.append(both)
     down_copies = []
     for t in range(chunks_out):
-        span = pl.ds(t * w_out, w_out)
+        span = pl.ds(*spans_out[t])
         copy = pltpu.make_async_copy(wd_hbm.at[:, :, span], wd.at[:, :, span], d_sem.at[t])
         copy.start()
         down_copies.append(copy)
@@ -75,12 +79,23 @@
     )
 
     for t in range(chunks_in):
+        at, w_in = spans_in[t]
+        v_in = w_in // pieces
         own = [
-            x_ref[:, t * w_in + j * v_in : t * w_in + (j + 1) * v_in].astype(F32)
-            for j in range(pieces)
+            x_ref[:, at + j * v_in : at + (j + 1) * v_in].astype(F32) for j in range(pieces)
         ]
-        zin[t, p] = jnp.concatenate(own, axis=0).astype(BF16)
-    zgate[p] = jnp.concatenate([g_ref[...]] * pieces, axis=0).astype(BF16)
+        zins[t][p] = jnp.concatenate(own, axis=0).astype(BF16)
+    column = lax.broadcasted_iota(jnp.int32, (1, GATE_COLS), 1)
+    gate_rows = []
+    for r in range(rows):
+        line = jnp.zeros((1, GATE_COLS), F32)
+        values = g_ref[r].astype(F32)
+        for j in range(r_ref.shape[1]):
+            for e in range(EXP_NODE):
+                hit = column == r_ref[r : r + 1, j : j + 1] * EXP_NODE + e
+                line = jnp.where(hit, values[j : j + 1, e : e + 1], line)
+        gate_rows.append(line)
+    zgate[p] = jnp.concatenate(gate_rows * pieces, axis=0).astype(BF16)
 
     pl.semaphore_wait(barrier, peers - 1 + xs - 1 + 1)
 
@@ -110,7 +125,7 @@
 
     for t in range(chunks_in):
         for d in range(1, peers):
-            send(zin.at[t, p], zin.at[t, p], zs.at[t, d - 1], zr.at[t, d - 1], to_peer(d))
+            send(zins[t].at[p], zins[t].at[p], zs.at[t, d - 1], zr.at[t, d - 1], to_peer(d))
     for d in range(1, peers):
         send(zgate.at[p], zgate.at[p], gzs.at[d - 1], gzr.at[d - 1], to_peer(d))
 
@@ -123,26 +138,28 @@
 
     def place(t):
         for d in range(1, peers):
-            arrived(zin.at[t, peer_of(peers - d)], zs.at[t, d - 1], zr.at[t, d - 1], to_peer(d))
-        stacked = zin[t].reshape(peers * SLOT, v_in)
+            arrived(zins[t].at[peer_of(peers - d)], zs.at[t, d - 1], zr.at[t, d - 1], to_peer(d))
+        gin = gins[t]
+        v_in = spans_in[t][1] // pieces
+        stacked = zins[t][...].reshape(peers * SLOT, v_in)
         for j in range(pieces):
-            gin[t, c, xi, :, j * v_in : (j + 1) * v_in] = jnp.dot(
+            gin[c, xi, :, j * v_in : (j + 1) * v_in] = jnp.dot(
                 spread(j), stacked, preferred_element_type=F32
             ).astype(BF16)
         for d in range(1, xs):
-            send(gin.at[t, c, xi], gin.at[t, c, xi], xs_s.at[t, d - 1], xs_r.at[t, d - 1], to_x(d))
-        send(gin.at[t, c, xi], gin.at[t, c, xi], cs.at[t, 0], cr.at[t, 0], to_core)
+            send(gin.at[c, xi], gin.at[c, xi], xs_s.at[t, d - 1], xs_r.at[t, d - 1], to_x(d))
+        send(gin.at[c, xi], gin.at[c, xi], cs.at[t, 0], cr.at[t, 0], to_core)
 
     def forward(t):
         for d in range(1, xs):
             other = x_of(xs - d)
-            block = gin.at[t, c, other]
+            block = gins[t].at[c, other]
             arrived(block, xs_s.at[t, d - 1], xs_r.at[t, d - 1], to_x(d))
             send(block, block, cs.at[t, d], cr.at[t, d], to_core)
 
     def gathered(t):
         for d in range(xs):
-            block = gin.at[t, 1 - c, x_of(xs - d)]
+            block = gins[t].at[1 - c, x_of(xs - d)]
             arrived(block, cs.at[t, d], cr.at[t, d], to_core)
 
     all_rows = CORES * xs * node_rows
@@ -151,11 +168,12 @@
         gathered(t)
         for copy in weight_copies[t]:
             copy.wait()
-        lhs = gin[t].reshape(all_rows, w_in)
+        at, w_in = spans_in[t]
+        lhs = gins[t][...].reshape(all_rows, w_in)
         for e in range(EXP_NODE):
             for i, w in enumerate((wg, wu)):
                 value = jnp.dot(
-                    lhs, w[e, t * w_in : (t + 1) * w_in, :], preferred_element_type=F32
+                    lhs, w[e, at : at + w_in, :], preferred_element_type=F32
                 )
                 if t == 0:
                     acc[e, i] = value
@@ -200,20 +218,21 @@
     def second_half(t):
         down_copies[t].wait()
         total = None
+        at, w_out = spans_out[t]
         for e in range(EXP_NODE):
             value = row_gates[e] * jnp.dot(
-                hid[e], wd[e, :, t * w_out : (t + 1) * w_out], preferred_element_type=F32
+                hid[e], wd[e, :, at : at + w_out], preferred_element_type=F32
             )
             total = value if total is None else total + value
-        part[t] = total.astype(BF16).reshape(CORES, xs, node_rows, w_out)
-        send(part.at[t, 1 - c], cbuf.at[t], ocs.at[t], ocr.at[t], to_core)
+        parts[t][...] = total.astype(BF16).reshape(CORES, xs, node_rows, w_out)
+        send(parts[t].at[1 - c], cbufs[t], ocs.at[t], ocr.at[t], to_core)
 
     def core_sum(t):
-        arrived(cbuf.at[t], ocs.at[t], ocr.at[t], to_core)
-        xsum[t] = (part[t, c].astype(F32) + cbuf[t].astype(F32)).astype(BF16)
+        arrived(cbufs[t], ocs.at[t], ocr.at[t], to_core)
+        xsums[t][...] = (parts[t][c].astype(F32) + cbufs[t][...].astype(F32)).astype(BF16)
         for d in range(1, xs):
             send(
-                xsum.at[t, x_of(d)], xbuf.at[t, d - 1],
+                xsums[t].at[x_of(d)], xbufs[t].at[d - 1],
                 oxs.at[t, d - 1], oxr.at[t, d - 1], to_x(d),
             )
 
@@ -222,10 +241,11 @@
     slot_base = (row_of // rows) * SLOT + row_of % rows
 
     def node_sum(t):
-        value = xsum[t, xi].astype(F32)
+        v_out = spans_out[t][1] // pieces
+        value = xsums[t][xi].astype(F32)
         for d in range(1, xs):
-            arrived(xbuf.at[t, d - 1], oxs.at[t, d - 1], oxr.at[t, d - 1], to_x(d))
-            value = value + xbuf[t, d - 1].astype(F32)
+            arrived(xbufs[t].at[d - 1], oxs.at[t, d - 1], oxr.at[t, d - 1], to_x(d))
+            value = value + xbufs[t][d - 1].astype(F32)
         value = value.astype(BF16)
         slots = None
         for j in range(pieces):
@@ -234,26 +254,28 @@
                 gather, value[:, j * v_out : (j + 1) * v_out], preferred_element_type=F32
             )
             slots = piece if slots is None else slots + piece
-        zout[t] = slots.astype(BF16).reshape(peers, SLOT, v_out)
+        zouts[t][...] = slots.astype(BF16).reshape(peers, SLOT, v_out)
         for d in range(1, peers):
             send(
-                zout.at[t, peer_of(d)], zbuf.at[t, d - 1],
+                zouts[t].at[peer_of(d)], zbufs[t].at[d - 1],
                 ozs.at[t, d - 1], ozr.at[t, d - 1], to_peer(d),
             )
 
     def finish(t):
-        value = zout[t, p].astype(F32)
+        at, w_out = spans_out[t]
+        v_out = w_out // pieces
+        value = zouts[t][p].astype(F32)
         for d in range(1, peers):
-            arrived(zbuf.at[t, d - 1], ozs.at[t, d - 1], ozr.at[t, d - 1], to_peer(d))
-            value = value + zbuf[t, d - 1].astype(F32)
+            arrived(zbufs[t].at[d - 1], ozs.at[t, d - 1], ozr.at[t, d - 1], to_peer(d))
+            value = value + zbufs[t][d - 1].astype(F32)
         for j in range(pieces):
-            out_ref[:, t * w_out + j * v_out : t * w_out + (j + 1) * v_out] = value[
+            out_ref[:, at + j * v_out : at + (j + 1) * v_out] = value[
                 j * rows : (j + 1) * rows
             ].astype(BF16)
 
     steps = (second_half, core_sum, node_sum, finish)
-    for t in range(chunks_out + len(steps) - 1):
-        for lag, step in enumerate(steps):
+    for t in range(chunks_out + LAGS[-1]):
+        for lag, step in zip(LAGS, steps):
             if 0 <= t - lag < chunks_out:
                 step(t - lag)
 
@@ -270,16 +292,9 @@
     pieces = SLOT // rows
     node_rows = peers * rows
     all_rows = node_count * node_rows
-    ti, to = CHUNKS_IN, CHUNKS_OUT
-    wi, wo = width // ti, width // to
-    vi, vo = wi // pieces, wo // pieces
-
-    column = jnp.arange(GATE_COLS, dtype=jnp.int32)[None, :]
-    gate_matrix = jnp.zeros((rows, GATE_COLS), F32)
-    for j in range(route_nodes.shape[1]):
-        for e in range(EXP_NODE):
-            hit = column == route_nodes[:, j : j + 1] * EXP_NODE + e
-            gate_matrix = jnp.where(hit, gates[:, j, e : e + 1].astype(F32), gate_matrix)
+    spans_in = chunks_of(width, PARTS_IN)
+    spans_out = chunks_of(width, PARTS_OUT)
+    ti, to = len(spans_in), len(spans_out)
 
     vmem = pl.BlockSpec(memory_space=pltpu.VMEM)
     hbm = pl.BlockSpec(memory_space=pl.ANY)
@@ -290,18 +305,18 @@
         pltpu.VMEM(w_gate.shape, BF16),
         pltpu.VMEM(w_up.shape, BF16),
         pltpu.VMEM(w_down.shape, BF16),
-        pltpu.VMEM((ti, peers, SLOT, vi), BF16),
-        pltpu.VMEM((ti, CORES, xs, node_rows, wi), BF16),
+        [pltpu.VMEM((peers, SLOT, w // pieces), BF16) for _, w in spans_in],
+        [pltpu.VMEM((CORES, xs, node_rows, w), BF16) for _, w in spans_in],
         pltpu.VMEM((peers, SLOT, GATE_COLS), BF16),
         pltpu.VMEM((CORES, xs, node_rows, GATE_COLS), BF16),
         pltpu.VMEM((EXP_NODE, 2, all_rows, hidden), F32),
         pltpu.VMEM((EXP_NODE, all_rows, hidden), BF16),
-        pltpu.VMEM((to, CORES, xs, node_rows, wo), BF16),
-        pltpu.VMEM((to, xs, node_rows, wo), BF16),
-        pltpu.VMEM((to, xs, node_rows, wo), BF16),
-        pltpu.VMEM((to, xfar, node_rows, wo), BF16),
-        pltpu.VMEM((to, peers, SLOT, vo), BF16),
-        pltpu.VMEM((to, far, SLOT, vo), BF16),
+        [pltpu.VMEM((CORES, xs, node_rows, w), BF16) for _, w in spans_out],
+        [pltpu.VMEM((xs, node_rows, w), BF16) for _, w in spans_out],
+        [pltpu.VMEM((xs, node_rows, w), BF16) for _, w in spans_out],
+        [pltpu.VMEM((xfar, node_rows, w), BF16) for _, w in spans_out],
+        [pltpu.VMEM((peers, SLOT, w // pieces), BF16) for _, w in spans_out],
+        [pltpu.VMEM((far, SLOT, w // pieces), BF16) for _, w in spans_out],
         dma((ti, 2)), dma((to,)),
         dma((ti, far)), dma((ti, far)), dma((ti, xfar)), dma((ti, xfar)),
         dma((ti, xs)), dma((ti, xs)),
@@ -310,9 +325,9 @@
     ]
     weight_count = w_gate.size + w_up.size + w_down.size
     return pl.pallas_call(
-        functools.partial(kernel, peers, xs, rows, ti, to),
+        functools.partial(kernel, peers, xs, rows, spans_in, spans_out),
         out_shape=jax.ShapeDtypeStruct((rows, width), BF16),
-        in_specs=[vmem, vmem, hbm, hbm, hbm],
+        in_specs=[vmem, vmem, vmem, hbm, hbm, hbm],
         out_specs=vmem,
         scratch_shapes=scratch,
         compiler_params=pltpu.CompilerParams(
@@ -323,7 +338,7 @@
             bytes_accessed=2 * weight_count,
             transcendentals=EXP_NODE * all_rows * hidden,
         ),
-    )(moe_rows, gate_matrix, w_gate, w_up, w_down)
+    )(moe_rows, route_nodes, gates, w_gate, w_up, w_down)
 
 
 def solution(mesh):

time: 40.4 us -> 39.1 us (0.968)
  local copies, waits for them, and re-layouts: 1.46 us -> 4.14 us
  other arithmetic: 2.15 us -> 0 us
  Pallas kernels: 36.6 us -> 34.7 us
    unnamed x1 -> x3, local copies, waits for them, and re-layouts: 1.46 us -> 4.14 us
    pallas_call x1, Pallas kernels: 36.6 us -> 34.7 us  [on_device(): pl.pallas_call(functools.partial(kernel, peers, xs, rows, spans_in, spans...]
    eq x1 -> x0, other arithmetic: 0.76 us -> none  [on_device(): hit = column == route_nodes[:, j:j + 1] * EXP_NODE + e]
    convert_element_type x1 -> x0, other arithmetic: 0.74 us -> none  [on_device(): gate_matrix = jnp.where(hit, gates[:, j, e:e + 1].astype(F32), gate_matrix)]
    select_n x1 -> x0, other arithmetic: 0.65 us -> none  [on_device(): gate_matrix = jnp.where(hit, gates[:, j, e:e + 1].astype(F32), gate_matrix)]
where the time goes in v2:
time: 39.1 us; the launch traced here: 38.9 us
  Pallas kernels  34.7 us (89%)
  local copies, waits for them, and re-layouts  4.14 us (11%)
    pallas_call x1, Pallas kernels, on_device(): pl.pallas_call(functools.partial(kernel, peers, xs, rows, spans_in, spans...  34.7 us
    unnamed x3, local copies, waits for them, and re-layouts  4.14 us

profile of v2, /device:TPU:0, one launch (start us, length us, event | category | flops | bytes accessed | tf_op | source)
XLA Modules:
  0.0 38.9 jit_solution(10208058615084896817)
XLA Ops:
  0.0 1.3 %copy.7.r_ref = s32[4,2]{1,0:T(4,128)} copy(s32[4,2]{0,1:T(2,128)} %param.7) | data formatting | bytes 64 | tf_op args[1]
  1.3 1.3 %copy.8.g_ref = bf16[4,2,2]{2,1,0:T(2,128)(2,1)} copy(bf16[4,2,2]{0,2,1:T(2,128)(2,1)} %param.8) | data formatting | bytes 64 | tf_op args[2]
  2.7 34.7 %shard_map.64 = bf16[4,7168]{1,0:T(4,128)(2,1)} custom-call(bf16[4,7168]{1,0:T(4,128)(2,1)} %x_ref.1, s32[4,2]{1,0:T(4,128)} %copy.7.r_ref, bf16[4,2,2]{2,1,0:T(2,128)(2,1)} %copy.8.g_ref, bf16[2,7168,512]{2,1,0:T(8,128)(2,1)} %wg_hbm.1, bf16[2,7168,512]{2,1,0:T(8,128)(2,1)} %wu_hbm.1, bf16[2,512,7168]{2,1,0:T(8,128)(2,1)} %wd_hbm.1), custom_call_target="tpu_custom_call" | custom-call | flops 2818572288 | bytes 44040192 | tf_op jit(solution)/shard_map/pallas_call | solution.py:327
  37.4 1.5 %copy.10 = bf16[4,7168]{1,0:T(4,128)(2,1)} copy(bf16[4,7168]{1,0:T(4,128)(2,1)} %shard_map.64) | data formatting | bytes 114688

commit v3 on v2

--- a/solution.py
+++ b/solution.py
@@ -13,7 +13,7 @@
 SLOT = 16
 GATE_COLS = 128
 UNIT = 512
-PARTS_IN = 4
+PARTS_IN = 7
 PARTS_OUT = 4
 LAGS = (0, 1, 3, 5)
 F32 = jnp.float32

time: 39.1 us -> 39.6 us (1.013)
  Pallas kernels: 34.7 us -> 35.2 us
    pallas_call x1, Pallas kernels: 34.7 us -> 35.2 us  [on_device(): pl.pallas_call(functools.partial(kernel, peers, xs, rows, spans_in, spans...]
where the time goes in v3:
time: 39.6 us; the launch traced here: 39.4 us
  Pallas kernels  35.2 us (89%)
  local copies, waits for them, and re-layouts  4.14 us (10%)
    pallas_call x1, Pallas kernels, on_device(): pl.pallas_call(functools.partial(kernel, peers, xs, rows, spans_in, spans...  35.2 us
    unnamed x3, local copies, waits for them, and re-layouts  4.14 us

profile of v3, /device:TPU:0, one launch (start us, length us, event | category | flops | bytes accessed | tf_op | source)
XLA Modules:
  0.0 39.4 jit_solution(8716957333933814702)
XLA Ops:
  0.0 1.3 %copy.7.r_ref = s32[4,2]{1,0:T(4,128)} copy(s32[4,2]{0,1:T(2,128)} %param.7) | data formatting | bytes 64 | tf_op args[1]
  1.3 1.3 %copy.8.g_ref = bf16[4,2,2]{2,1,0:T(2,128)(2,1)} copy(bf16[4,2,2]{0,2,1:T(2,128)(2,1)} %param.8) | data formatting | bytes 64 | tf_op args[2]
  2.7 35.2 %shard_map.64 = bf16[4,7168]{1,0:T(4,128)(2,1)} custom-call(bf16[4,7168]{1,0:T(4,128)(2,1)} %x_ref.1, s32[4,2]{1,0:T(4,128)} %copy.7.r_ref, bf16[4,2,2]{2,1,0:T(2,128)(2,1)} %copy.8.g_ref, bf16[2,7168,512]{2,1,0:T(8,128)(2,1)} %wg_hbm.1, bf16[2,7168,512]{2,1,0:T(8,128)(2,1)} %wu_hbm.1, bf16[2,512,7168]{2,1,0:T(8,128)(2,1)} %wd_hbm.1), custom_call_target="tpu_custom_call" | custom-call | flops 2818572288 | bytes 44040192 | tf_op jit(solution)/shard_map/pallas_call | solution.py:327
  37.9 1.5 %copy.10 = bf16[4,7168]{1,0:T(4,128)(2,1)} copy(bf16[4,7168]{1,0:T(4,128)(2,1)} %shard_map.64) | data formatting | bytes 114688
